TPU v7x, 32 devices: a whole 2x2x4 slice. The times are simulated.
32 devices in a mesh: cfg: 2 (over core), seq: 4 (over z), blk: 4 (over y, x).
Axes of the slice: x: 2, y: 2, z: 4, core: 2. Of those that a mesh axis runs over, the one named last changes fastest.
Arguments:
- img_hidden: bfloat16 [2, 2, 2048, 1536], P('cfg', None, 'seq', 'blk'), may hold values from -15 to 15
- txt_hidden: bfloat16 [2, 2, 160, 1536], P('cfg', None, 'seq', 'blk'), may hold values from -6 to 6
- img_mod: float32 [2, 2, 6, 1536], P('cfg'), may hold values from -9 to 9
- txt_mod: float32 [2, 2, 2, 1536], P('cfg'), may hold values from -3 to 3
- out_mod: float32 [2, 2, 2, 1536], P('cfg'), may hold values from -3 to 3
- w_qkv: bfloat16 [3, 1536, 1536], P(None, None, 'blk'), may hold values from -0.25 to 0.25
- w_txt_kv: bfloat16 [2, 1536, 1536], P(None, None, 'blk'), may hold values from -0.25 to 0.25
- w_out: bfloat16 [1536, 1536], P('blk'), may hold values from -0.15625 to 0.15625
- w_fc1: bfloat16 [1536, 6144], P(None, 'blk'), may hold values from -0.15625 to 0.15625
- w_fc2: bfloat16 [6144, 1536], P('blk'), may hold values from -0.078125 to 0.078125
- w_proj: bfloat16 [1536, 64], P('blk'), may hold values from -0.15625 to 0.15625
- latent: float32 [2, 2048, 64], P(None, 'seq', 'cfg'), may hold values from -6 to 6
- lengths: int32 [2, 2], P('cfg'), may hold values from 1 to 154, as said below
- t_index: int32 [2], replicated, may hold values from 0 to 24
- stride: int32 [2], replicated, may hold values from 1 to 4
- guide: float32 [2], replicated, may hold values from 4 to 8
Outputs:
- new_latent: float32 [2, 2048, 64], P(None, 'seq', 'cfg')
- update_max: float32 [2], replicated
Inputs may be any that keep to these rules, and one draw needn't show every extreme that they name: `lengths`: at least one entry equals 154.
All inputs are finite; a program needn't handle non-finite values.
Results may differ from a plain program's by a relative error of at most 0.015.
Values may be sent and summed in bfloat16 or wider, within the bound.
A program may use at most 192 MiB of HBM per device.

v0:
```python
import jax
import jax.numpy as jnp
from jax import lax
from jax.sharding import PartitionSpec as P

HEAD = 64
STEPS = 28
EPSILON = 1e-06
BLOCK_ROWS = 512


def from_partner(value, axis, bit):
    return lax.ppermute(value, axis, [(i, i ^ 1 << bit) for i in range(lax.axis_size(axis))])


def normalize(values):
    values = values.astype(jnp.float32)
    center = jnp.mean(values, axis=-1, keepdims=True)
    spread = jnp.mean(jnp.square(values - center), axis=-1, keepdims=True)
    return (values - center) * lax.rsqrt(spread + EPSILON)


def modulate(values, scale_row, shift_row):
    return (normalize(values) * (1.0 + scale_row[:, None, :]) + shift_row[:, None, :]).astype(
        jnp.bfloat16
    )


def project(values, weight):
    flat_rows = values.reshape(-1, values.shape[-1])
    result = jnp.dot(flat_rows, weight, preferred_element_type=jnp.float32)
    return result.reshape(values.shape[:-1] + (weight.shape[-1],))


def noise_level(step_index):
    remain = 1.0 - step_index.astype(jnp.float32) / STEPS
    return 3.0 * remain / (1.0 + 2.0 * remain)


def own_columns(values, column_block, shard_width):
    return lax.dynamic_slice_in_dim(
        values, column_block * shard_width, shard_width, values.ndim - 1
    )


def per_device(
    img_hidden,
    txt_hidden,
    img_mod,
    txt_mod,
    out_mod,
    w_qkv,
    w_txt_kv,
    w_out,
    w_fc1,
    w_fc2,
    w_proj,
    latent,
    lengths,
    t_index,
    stride,
    guide,
):
    column_block = lax.axis_index("blk")
    shard_width = img_hidden.shape[3]
    model_width = shard_width * lax.axis_size("blk")
    image_full, text_full = (
        lax.all_gather(img_hidden[0], "blk", axis=2, tiled=True),
        lax.all_gather(txt_hidden[0], "blk", axis=2, tiled=True),
    )
    image_mod = img_mod[0]
    prompts = image_full.shape[0]
    img_rows = image_full.shape[1]
    attn_in = modulate(image_full, image_mod[:, 1], image_mod[:, 0])
    queries = project(attn_in, w_qkv[0]).astype(jnp.bfloat16)
    keys_img = project(attn_in, w_qkv[1]).astype(jnp.bfloat16)
    values_img = project(attn_in, w_qkv[2]).astype(jnp.bfloat16)
    text_norm = modulate(text_full, txt_mod[0][:, 0], txt_mod[0][:, 1])
    text_keys = project(text_norm, w_txt_kv[0]).astype(jnp.bfloat16)
    text_values = project(text_norm, w_txt_kv[1]).astype(jnp.bfloat16)
    head_width = queries.shape[2]
    head_count = head_width // HEAD
    query_heads = queries.reshape(prompts, img_rows, head_count, HEAD)
    text_limit = lengths[0]

    def attend_block(running_state, key_block, value_block, live_mask):
        accumulated, running, denominator = running_state
        key_count = key_block.shape[1]
        key_heads = key_block.reshape(prompts, key_count, head_count, HEAD)
        value_heads = value_block.reshape(prompts, key_count, head_count, HEAD)
        scores = jnp.einsum(
            "pqhe,pkhe->phqk", query_heads, key_heads, preferred_element_type=jnp.float32
        ) * HEAD ** (-0.5)
        if live_mask is not None:
            scores = jnp.where(live_mask[:, None, None, :], scores, -jnp.inf)
        updated = jnp.maximum(running, jnp.max(scores, axis=-1))
        factor = jnp.exp(running - updated)
        weights = jnp.exp(scores - updated[..., None])
        denominator = denominator * factor + jnp.sum(weights, axis=-1)
        mixed_values = jnp.einsum(
            "phqk,pkhe->phqe",
            weights.astype(jnp.bfloat16),
            value_heads,
            preferred_element_type=jnp.float32,
        )
        accumulated = accumulated * factor[..., None] + mixed_values
        return (accumulated, updated, denominator)

    initial = (
        jnp.zeros((prompts, head_count, img_rows, HEAD), jnp.float32),
        jnp.full((prompts, head_count, img_rows), -1e30, jnp.float32),
        jnp.zeros((prompts, head_count, img_rows), jnp.float32),
    )
    running_state = initial
    key_piece = lax.all_gather(keys_img, "seq", axis=1, tiled=True)
    value_piece = lax.all_gather(values_img, "seq", axis=1, tiled=True)
    key_count = key_piece.shape[1]
    blocks = key_count // BLOCK_ROWS
    key_split = key_piece.reshape(prompts, blocks, BLOCK_ROWS, head_width).transpose(1, 0, 2, 3)
    value_split = value_piece.reshape(prompts, blocks, BLOCK_ROWS, head_width).transpose(1, 0, 2, 3)

    def scan_step(state_now, operands):
        key_block, value_block = operands
        return (attend_block(state_now, key_block, value_block, None), None)

    running_state, unused = lax.scan(scan_step, running_state, (key_split, value_split))
    all_text_keys, all_text_values = (
        lax.all_gather(text_keys, "seq", axis=1, tiled=True),
        lax.all_gather(text_values, "seq", axis=1, tiled=True),
    )
    slot_index = jnp.arange(all_text_keys.shape[1], dtype=jnp.int32)
    text_mask = slot_index[None, :] < text_limit[:, None]
    accumulated, running, denominator = attend_block(
        running_state, all_text_keys, all_text_values, text_mask
    )
    attended = (accumulated / denominator[..., None]).astype(jnp.bfloat16)
    attended = attended.transpose(0, 2, 1, 3).reshape(prompts, img_rows, head_width)
    attn_part = project(attended, w_out)
    attn_sum = lax.psum(attn_part.astype(jnp.bfloat16), "blk").astype(jnp.float32)
    resid_full = (image_full.astype(jnp.float32) + image_mod[:, 2][:, None, :] * attn_sum).astype(
        jnp.bfloat16
    )
    resid_one = own_columns(resid_full, column_block, shard_width)
    mlp_in = modulate(resid_full, image_mod[:, 4], image_mod[:, 3])
    hidden_units = jax.nn.gelu(project(mlp_in, w_fc1), approximate=True).astype(jnp.bfloat16)
    mlp_sum = lax.psum_scatter(
        project(hidden_units, w_fc2).astype(jnp.bfloat16), "blk", scatter_dimension=2, tiled=True
    ).astype(jnp.float32)
    gate_mlp = own_columns(image_mod[:, 5], column_block, shard_width)
    resid_two = (resid_one.astype(jnp.float32) + gate_mlp[:, None, :] * mlp_sum).astype(
        jnp.bfloat16
    )
    stream = resid_two.astype(jnp.float32)
    row_sum, row_squares = lax.psum(
        (jnp.sum(stream, axis=-1), jnp.sum(stream * stream, axis=-1)), "blk"
    )
    center = row_sum / model_width
    spread = row_squares / model_width - center * center
    final_mod = out_mod[0]
    final_scale = own_columns(final_mod[:, 0], column_block, shard_width)
    final_shift = own_columns(final_mod[:, 1], column_block, shard_width)
    final_in = (
        (stream - center[..., None])
        * lax.rsqrt(spread[..., None] + EPSILON)
        * (1.0 + final_scale[:, None, :])
        + final_shift[:, None, :]
    ).astype(jnp.bfloat16)
    velocity_part = project(final_in, w_proj)
    half_index = lax.axis_index("cfg")
    channel_width = latent.shape[2]
    guide_scale = guide[:, None, None]
    velocity = lax.psum(velocity_part.astype(jnp.bfloat16), "blk").astype(jnp.float32)
    outgoing = own_columns(velocity, 1 - half_index, channel_width)
    other_half = from_partner(outgoing.astype(jnp.bfloat16), "cfg", 0).astype(outgoing.dtype)
    own_half = own_columns(velocity, half_index, channel_width)
    velocity_cond = jnp.where(half_index == 0, own_half, other_half)
    velocity_uncond = jnp.where(half_index == 0, other_half, own_half)
    guided = velocity_uncond + guide_scale * (velocity_cond - velocity_uncond)
    step_size = noise_level(t_index + stride) - noise_level(t_index)
    update = step_size[:, None, None] * guided
    new_latent = latent + update
    local_peak = jnp.max(jnp.abs(update), axis=(1, 2))
    peak_value = lax.pmax(local_peak, ("cfg", "seq"))
    return (new_latent, peak_value)


def solution(mesh):
    placed = (
        P("cfg", None, "seq", "blk"),
        P("cfg", None, "seq", "blk"),
        P("cfg", None, None, None),
        P("cfg", None, None, None),
        P("cfg", None, None, None),
        P(None, None, "blk"),
        P(None, None, "blk"),
        P("blk", None),
        P(None, "blk"),
        P("blk", None),
        P("blk", None),
        P(None, "seq", "cfg"),
        P("cfg", None),
        P(),
        P(),
        P(),
    )
    return jax.shard_map(
        per_device,
        mesh=mesh,
        in_specs=placed,
        out_specs=(P(None, "seq", "cfg"), P()),
        check_vma=False,
    )
```

profile of v0, /device:TPU:0, one launch (start us, length us, event | category | flops | bytes accessed | tf_op | source)
XLA Modules:
  0.0 552.0 jit_solution(2850391820597721948)
XLA Ops:
  8.0 0.9 copy.69
  9.6 46.8 %all-gather.10.cloned.1.call-done = bf16[1,2,512,1536]{3,2,1,0:T(8,128)(2,1)} async-done(((bf16[1,2,512,384]{3,2,1,0:T(8,128)(2,1)}), bf16[1,2,512,1536]{3,2,1,0:T(8,128)(2,1)}) %all-gather.10.cloned.1.call-update) | async-done | bytes 3145744 | tf_op jit(solution)/shard_map/all_gather | solution.py:68
  56.4 2.5 convert_reduce_fusion
  59.2 1.0 fusion.18
  60.2 4.0 convolution_convert_fusion.1
  64.4 5.0 convolution_convert_fusion.3
  69.5 9.2 %all-gather.1 = bf16[1,2,40,1536]{3,2,1,0:T(8,128)(2,1)S(1)} all-gather(bf16[1,2,40,384]{3,2,1,0:T(8,128)(2,1)S(1)} %copy-done.12), channel_id=3, replica_groups=mesh['cfg'=2,'seq'=4,'blk'=4] {'blk'}, dimensions={3}, use_global_device_ids=true | all-gather | bytes 307200 | tf_op jit(solution)/shard_map/all_gather | solution.py:69
  79.1 1.7 fusion.79
  80.8 16.4 %all_gather.22 = bf16[2,160,384]{2,1,0:T(8,128)(2,1)} all-gather(bf16[2,40,384]{2,1,0:T(8,128)(2,1)S(1)} %fusion.79), channel_id=1, replica_groups=mesh['cfg'=2,'seq'=4,'blk'=4] {'seq'}, dimensions={1}, use_global_device_ids=true | all-gather | bytes 307200 | tf_op jit(solution)/shard_map/all_gather | solution.py:128
  97.2 1.1 copy.39
  98.3 1.7 fusion.82
  100.0 16.7 %all_gather.23 = bf16[2,160,384]{2,1,0:T(8,128)(2,1)S(1)} all-gather(bf16[2,40,384]{2,1,0:T(8,128)(2,1)S(1)} %fusion.82), channel_id=1, replica_groups=mesh['cfg'=2,'seq'=4,'blk'=4] {'seq'}, dimensions={1}, use_global_device_ids=true | all-gather | bytes 307200 | tf_op jit(solution)/shard_map/all_gather | solution.py:129
  116.6 0.9 copy.40
  117.6 4.0 convolution_convert_fusion.2
  121.7 0.9 copy-done.2
  122.5 3.4 fusion.41
  125.9 9.6 %all-gather.8.cloned.1.call-done = bf16[2,2048,384]{2,1,0:T(8,128)(2,1)} async-done(((bf16[2,512,384]{2,1,0:T(8,128)(2,1)}), bf16[2,2048,384]{2,1,0:T(8,128)(2,1)}) %all-gather.8.cloned.1.call-update) | async-done | bytes 3145744 | tf_op jit(solution)/shard_map/all_gather | solution.py:116
  135.5 4.7 copy.38
  140.2 59.2 %all-gather.6.cloned.1.call-done = bf16[2,2048,384]{2,1,0:T(8,128)(2,1)} async-done(((bf16[2,512,384]{2,1,0:T(8,128)(2,1)}), bf16[2,2048,384]{2,1,0:T(8,128)(2,1)}) %all-gather.6.cloned.1.call-update) | async-done | bytes 3145744 | tf_op jit(solution)/shard_map/all_gather | solution.py:115
  199.4 4.7 copy.36
  204.1 87.5 %while.15 = (s32[]{:T(128)}, f32[2,6,512,64]{2,3,1,0:T(8,128)S(1)}, f32[2,6,512]{2,1,0:T(8,128)}, f32[2,6,512]{2,1,0:T(8,128)}, bf16[4,2,512,384]{2,3,1,0:T(8,12...) while((s32[]{:T(128)}, f32[2,6,512,64]{2,3,1,0:T(8,128)S(1)}, ...), condition=%wide.region_5.0_spmd.clone, body=%wide.region_2.5_spmd.clone.sunk | while | flops 831682560 | bytes 97419496 | solution.py:126
  204.1 1.5 constant_dynamic-slice_fusion.5
  205.5 8.1 %bitcast_reduce_fusion.2 = (f32[2,6,512]{2,1,0:T(8,128)}, f32[2,6,512,512]{3,2,1,0:T(8,128)}) fusion(bf16[2,512,6,64]{1,3,2,0:T(8,128)(2,1)S(1)} %bitcast.165, bf16[2,512,6,64]{1,3,2,0:T(8,128)(2,1)} %get-tuple-element.199), kind=kOutput, calls=%fused_computation.1.clone.1 | convolution fusion | flops 408938496 | bytes 14180352 | tf_op jit(solution)/shard_map/while/body/eval_jaxpr/pqhe,pkhe->phqk/dot_general | solution.py:91
  214.4 6.8 %fusion.134 = f32[2,6,512]{2,1,0:T(8,128)S(1)} fusion(f32[2,6,512,512]{3,2,1,0:T(8,128)} %get-tuple-element.172, f32[2,6,512]{2,1,0:T(8,128)S(1)} %select_maximum_fusion.2), kind=kLoop, calls=%fused_computation.3.clone.1 | loop fusion | flops 9431040 | bytes 12632064 | tf_op jit(solution)/shard_map/while/body/eval_jaxpr/reduce_sum | solution.py:99
  221.3 1.3 copy-done.1
  222.6 2.7 fusion.136
  225.9 1.5 constant_dynamic-slice_fusion.5
  227.4 8.1 %bitcast_reduce_fusion.2 = (f32[2,6,512]{2,1,0:T(8,128)}, f32[2,6,512,512]{3,2,1,0:T(8,128)}) fusion(bf16[2,512,6,64]{1,3,2,0:T(8,128)(2,1)S(1)} %bitcast.165, bf16[2,512,6,64]{1,3,2,0:T(8,128)(2,1)} %get-tuple-element.199), kind=kOutput, calls=%fused_computation.1.clone.1 | convolution fusion | flops 408938496 | bytes 14180352 | tf_op jit(solution)/shard_map/while/body/eval_jaxpr/pqhe,pkhe->phqk/dot_general | solution.py:91
  235.5 0.8 select_maximum_fusion.2
  236.3 6.8 %fusion.134 = f32[2,6,512]{2,1,0:T(8,128)S(1)} fusion(f32[2,6,512,512]{3,2,1,0:T(8,128)} %get-tuple-element.172, f32[2,6,512]{2,1,0:T(8,128)S(1)} %select_maximum_fusion.2), kind=kLoop, calls=%fused_computation.3.clone.1 | loop fusion | flops 9431040 | bytes 12632064 | tf_op jit(solution)/shard_map/while/body/eval_jaxpr/reduce_sum | solution.py:99
  243.2 1.3 copy-done.1
  244.5 2.7 fusion.136
  247.8 1.5 constant_dynamic-slice_fusion.5
  249.3 8.1 %bitcast_reduce_fusion.2 = (f32[2,6,512]{2,1,0:T(8,128)}, f32[2,6,512,512]{3,2,1,0:T(8,128)}) fusion(bf16[2,512,6,64]{1,3,2,0:T(8,128)(2,1)S(1)} %bitcast.165, bf16[2,512,6,64]{1,3,2,0:T(8,128)(2,1)} %get-tuple-element.199), kind=kOutput, calls=%fused_computation.1.clone.1 | convolution fusion | flops 408938496 | bytes 14180352 | tf_op jit(solution)/shard_map/while/body/eval_jaxpr/pqhe,pkhe->phqk/dot_general | solution.py:91
  257.4 0.8 select_maximum_fusion.2
  258.2 6.8 %fusion.134 = f32[2,6,512]{2,1,0:T(8,128)S(1)} fusion(f32[2,6,512,512]{3,2,1,0:T(8,128)} %get-tuple-element.172, f32[2,6,512]{2,1,0:T(8,128)S(1)} %select_maximum_fusion.2), kind=kLoop, calls=%fused_computation.3.clone.1 | loop fusion | flops 9431040 | bytes 12632064 | tf_op jit(solution)/shard_map/while/body/eval_jaxpr/reduce_sum | solution.py:99
  265.1 1.3 copy-done.1
  266.4 2.7 fusion.136
  269.7 1.5 constant_dynamic-slice_fusion.5
  271.2 8.1 %bitcast_reduce_fusion.2 = (f32[2,6,512]{2,1,0:T(8,128)}, f32[2,6,512,512]{3,2,1,0:T(8,128)}) fusion(bf16[2,512,6,64]{1,3,2,0:T(8,128)(2,1)S(1)} %bitcast.165, bf16[2,512,6,64]{1,3,2,0:T(8,128)(2,1)} %get-tuple-element.199), kind=kOutput, calls=%fused_computation.1.clone.1 | convolution fusion | flops 408938496 | bytes 14180352 | tf_op jit(solution)/shard_map/while/body/eval_jaxpr/pqhe,pkhe->phqk/dot_general | solution.py:91
  279.3 0.8 select_maximum_fusion.2
  280.1 6.8 %fusion.134 = f32[2,6,512]{2,1,0:T(8,128)S(1)} fusion(f32[2,6,512,512]{3,2,1,0:T(8,128)} %get-tuple-element.172, f32[2,6,512]{2,1,0:T(8,128)S(1)} %select_maximum_fusion.2), kind=kLoop, calls=%fused_computation.3.clone.1 | loop fusion | flops 9431040 | bytes 12632064 | tf_op jit(solution)/shard_map/while/body/eval_jaxpr/reduce_sum | solution.py:99
  287.0 1.3 copy-done.1
  288.3 2.7 fusion.136
  291.6 0.9 max.8
  292.5 3.4 fusion.47
  295.9 2.2 divide_convert_fusion
  298.1 3.5 convolution_convert_fusion
  301.8 85.9 %all-reduce.4.cloned.1.call-done = bf16[2,512,1536]{2,1,0:T(8,128)(2,1)} async-done(((bf16[2,512,1536]{2,1,0:T(8,128)(2,1)}), bf16[2,512,1536]{2,1,0:T(8,128)(2,1)}) %all-reduce.4.cloned.1.call-update) | async-done | bytes 3145744 | tf_op jit(solution)/shard_map/psum | solution.py:139
  387.7 4.0 convert_reduce_fusion.1
  391.8 1.6 copy-done.4
  393.4 1.0 fusion.22
  394.4 15.8 %fusion.38 = bf16[2,512,1536]{2,1,0:T(8,128)(2,1)} fusion(bf16[1536,1536]{1,0:T(8,128)(2,1)} %param.27, bf16[1536,1536]{1,0:T(8,128)(2,1)} %param.26, bf16[2,512,1536]{2,1,0:T(8,128)(2,1)} %copy-done.4, f32[2,1536]{1,0:T(2,128)S(1)} %get-tuple-element.113, f32[2,1536]{1,0:T(2,128)S(1)} %get-tuple-element.114, f32[2,512]{1,0:T(2,128)S(1)} %add_rsqrt_fusion.1, ...), kind=kOutput, calls=%fused_computation.50 | convolution fusion | flops 9688842240 | bytes 15761408 | tf_op jit(solution)/shard_map/dot_general | solution.py:31
  410.2 8.7 %copy.44 = bf16[2,512,1536]{1,0,2:T(2,128)(2,1)} copy(bf16[2,512,1536]{2,1,0:T(8,128)(2,1)} %fusion.38) | data formatting | bytes 6291456
  418.9 4.4 copy.57
  424.2 43.3 %reduce-scatter.4.cloned.1.call-done = bf16[384,1024]{1,0:T(8,128)(2,1)} async-done(((bf16[1536,1024]{1,0:T(8,128)(2,1)}), bf16[384,1024]{1,0:T(8,128)(2,1)}) %reduce-scatter.4.cloned.1.call-update) | async-done | bytes 786448
  467.4 2.6 reshape.158
  470.7 1.7 convert_reduce_fusion.2
  472.4 9.1 %all-reduce = (f32[2,512]{1,0:T(2,128)S(1)}, f32[2,512]{1,0:T(2,128)S(1)}) all-reduce(f32[2,512]{1,0:T(2,128)S(1)} %get-tuple-element.69, f32[2,512]{1,0:T(2,128)S(1)} %get-tuple-element.68), channel_id=1, replica_groups=mesh['cfg'=2,'seq'=4,'blk'=4] {'blk'}, use_global_device_ids=true, to_apply=%region_17.18 | all-reduce | flops 2048 | bytes 16384 | tf_op jit(solution)/shard_map/psum | solution.py:154
  481.5 1.2 convolution_convert_fusion.4
  482.7 42.1 %all-reduce.6.cloned.1.call-done = bf16[2,512,64]{1,2,0:T(8,128)(2,1)} async-done(((bf16[2,512,64]{1,2,0:T(8,128)(2,1)}), bf16[2,512,64]{1,2,0:T(8,128)(2,1)}) %all-reduce.6.cloned.1.call-update) | async-done | bytes 131088 | tf_op jit(solution)/shard_map/psum | solution.py:172
  524.8 0.9 convert_element_type.117
  525.9 1.2 collective-permute-done
  527.9 17.2 %pmax.7 = f32[2]{0:T(128)} all-reduce(f32[2]{0:T(128)S(1)} %get-tuple-element.97), channel_id=1, replica_groups=mesh['cfg'=2,'seq'=4,'blk'=4] {'cfg','seq'}, use_global_device_ids=true, to_apply=%region_20.21 | all-reduce | flops 2 | bytes 16 | tf_op jit(solution)/shard_map/pmax | solution.py:183
  (114 shorter events, 8.3 us)
Async XLA Ops:
  7.2 291.0 %copy-start = (bf16[384,1536]{1,0:T(8,128)(2,1)S(1)}, bf16[384,1536]{1,0:T(8,128)(2,1)}, u32[]{:S(2)}) copy-start(bf16[384,1536]{1,0:T(8,128)(2,1)} %param.25) | copy-start | bytes 3538948
  7.2 49.2 %all-gather.10.cloned.1.call-start = ((), (), s32[]{:S(2)}) async-start(), calls=%async_computation.5 | async-start | bytes 3932160 | tf_op jit(solution)/shard_map/all_gather | solution.py:68
  7.9 127.6 %all-gather.8.cloned.1.call-start = ((), (), s32[]{:S(2)}) async-start(), calls=%async_computation.2 | async-start | bytes 3932160 | tf_op jit(solution)/shard_map/all_gather | solution.py:116
  56.4 2.8 copy-start.3
  64.3 5.2 copy-start.12
  64.3 14.7 %copy-start.15 = (f32[1,2,2,1536]{3,2,1,0:T(2,128)S(1)}, f32[1,2,2,1536]{3,2,1,0:T(2,128)}, u32[]{:S(2)}) copy-start(f32[1,2,2,1536]{3,2,1,0:T(2,128)} %param.21) | copy-start | bytes 73732
  64.3 135.0 %all-gather.6.cloned.1.call-start = ((), (), s32[]{:S(2)}) async-start(), calls=%async_computation.1 | async-start | bytes 3932160 | tf_op jit(solution)/shard_map/all_gather | solution.py:115
  69.3 48.2 %copy-start.19 = (s32[1,2]{1,0:T(1,128)S(1)}, s32[1,2]{1,0:T(1,128)}, u32[]{:S(2)}) copy-start(s32[1,2]{1,0:T(1,128)} %param.30) | copy-start | bytes 28
  69.4 318.3 %all-reduce.4.cloned.1.call-start = ((), (), s32[]{:S(2)}) async-start(), calls=%async_computation.3 | async-start | bytes 6291456 | tf_op jit(solution)/shard_map/psum | solution.py:139
  121.7 0.9 copy-start.2
  214.4 6.9 %copy-start.6 = (f32[2,6,512]{2,1,0:T(8,128)S(1)}, f32[2,6,512]{2,1,0:T(8,128)}, u32[]{:S(2)}) copy-start(f32[2,6,512]{2,1,0:T(8,128)} %get-tuple-element.187) | copy-start | bytes 73732 | tf_op jit(solution)/shard_map/while
  214.4 6.9 %copy-start.8 = (f32[2,6,512]{2,1,0:T(8,128)S(1)}, f32[2,6,512]{2,1,0:T(8,128)}, u32[]{:S(2)}) copy-start(f32[2,6,512]{2,1,0:T(8,128)} %get-tuple-element.188) | copy-start | bytes 73732 | tf_op jit(solution)/shard_map/while
  214.4 8.2 %copy-start.1 = (f32[2,6,512,512]{3,2,1,0:T(8,128)S(1)}, f32[2,6,512,512]{3,2,1,0:T(8,128)}, u32[]{:S(2)}) copy-start(f32[2,6,512,512]{3,2,1,0:T(8,128)} %get-tuple-element.172) | copy-start | bytes 37748740 | tf_op jit(solution)/shard_map/while
  221.3 4.0 copy-start.9
  236.3 6.8 %copy-start.6 = (f32[2,6,512]{2,1,0:T(8,128)S(1)}, f32[2,6,512]{2,1,0:T(8,128)}, u32[]{:S(2)}) copy-start(f32[2,6,512]{2,1,0:T(8,128)} %get-tuple-element.187) | copy-start | bytes 73732 | tf_op jit(solution)/shard_map/while
  236.3 6.9 %copy-start.8 = (f32[2,6,512]{2,1,0:T(8,128)S(1)}, f32[2,6,512]{2,1,0:T(8,128)}, u32[]{:S(2)}) copy-start(f32[2,6,512]{2,1,0:T(8,128)} %get-tuple-element.188) | copy-start | bytes 73732 | tf_op jit(solution)/shard_map/while
  236.3 8.2 %copy-start.1 = (f32[2,6,512,512]{3,2,1,0:T(8,128)S(1)}, f32[2,6,512,512]{3,2,1,0:T(8,128)}, u32[]{:S(2)}) copy-start(f32[2,6,512,512]{3,2,1,0:T(8,128)} %get-tuple-element.172) | copy-start | bytes 37748740 | tf_op jit(solution)/shard_map/while
  243.2 4.0 copy-start.9
  258.2 6.8 %copy-start.6 = (f32[2,6,512]{2,1,0:T(8,128)S(1)}, f32[2,6,512]{2,1,0:T(8,128)}, u32[]{:S(2)}) copy-start(f32[2,6,512]{2,1,0:T(8,128)} %get-tuple-element.187) | copy-start | bytes 73732 | tf_op jit(solution)/shard_map/while
  258.2 6.9 %copy-start.8 = (f32[2,6,512]{2,1,0:T(8,128)S(1)}, f32[2,6,512]{2,1,0:T(8,128)}, u32[]{:S(2)}) copy-start(f32[2,6,512]{2,1,0:T(8,128)} %get-tuple-element.188) | copy-start | bytes 73732 | tf_op jit(solution)/shard_map/while
  258.2 8.2 %copy-start.1 = (f32[2,6,512,512]{3,2,1,0:T(8,128)S(1)}, f32[2,6,512,512]{3,2,1,0:T(8,128)}, u32[]{:S(2)}) copy-start(f32[2,6,512,512]{3,2,1,0:T(8,128)} %get-tuple-element.172) | copy-start | bytes 37748740 | tf_op jit(solution)/shard_map/while
  265.1 4.0 copy-start.9
  280.1 6.8 %copy-start.6 = (f32[2,6,512]{2,1,0:T(8,128)S(1)}, f32[2,6,512]{2,1,0:T(8,128)}, u32[]{:S(2)}) copy-start(f32[2,6,512]{2,1,0:T(8,128)} %get-tuple-element.187) | copy-start | bytes 73732 | tf_op jit(solution)/shard_map/while
  280.1 6.9 %copy-start.8 = (f32[2,6,512]{2,1,0:T(8,128)S(1)}, f32[2,6,512]{2,1,0:T(8,128)}, u32[]{:S(2)}) copy-start(f32[2,6,512]{2,1,0:T(8,128)} %get-tuple-element.188) | copy-start | bytes 73732 | tf_op jit(solution)/shard_map/while
  280.1 8.2 %copy-start.1 = (f32[2,6,512,512]{3,2,1,0:T(8,128)S(1)}, f32[2,6,512,512]{3,2,1,0:T(8,128)}, u32[]{:S(2)}) copy-start(f32[2,6,512,512]{3,2,1,0:T(8,128)} %get-tuple-element.172) | copy-start | bytes 37748740 | tf_op jit(solution)/shard_map/while
  287.0 4.0 copy-start.9
  291.6 4.3 copy-start.7
  291.6 4.3 copy-start.10
  291.6 4.3 copy-start.5
  298.1 3.6 copy-start.13
  298.1 3.6 copy-start.14
  301.7 165.8 %reduce-scatter.4.cloned.1.call-start = ((), (), s32[]{:S(2)}) async-start(), calls=%async_computation.6 | async-start | bytes 3932160
  391.7 1.7 copy-start.4
  418.9 5.2 copy-start.16
  423.3 58.2 %copy-start.18 = (bf16[384,64]{0,1:T(8,128)(2,1)S(1)}, bf16[384,64]{0,1:T(8,128)(2,1)}, u32[]{:S(2)}) copy-start(bf16[384,64]{0,1:T(8,128)(2,1)} %param.28) | copy-start | bytes 147460
  423.3 101.5 %all-reduce.6.cloned.1.call-start = ((), (), s32[]{:S(2)}) async-start(), calls=%async_computation.4 | async-start | bytes 262144 | tf_op jit(solution)/shard_map/psum | solution.py:172
  424.1 101.7 %copy-start.20 = (s32[2]{0:T(128)S(1)}, s32[2]{0:T(128)}, u32[]{:S(2)}) copy-start(s32[2]{0:T(128)} %param.31) | copy-start | bytes 28
  424.2 101.7 %copy-start.21 = (s32[2]{0:T(128)S(1)}, s32[2]{0:T(128)}, u32[]{:S(2)}) copy-start(s32[2]{0:T(128)} %param.32) | copy-start | bytes 28
  424.2 103.0 %copy-start.11 = (f32[2,512,32]{1,2,0:T(8,128)S(1)}, f32[2,512,32]{1,2,0:T(8,128)}, u32[]{:S(2)}) copy-start(f32[2,512,32]{1,2,0:T(8,128)} %param.29) | copy-start | bytes 393220
  424.2 102.9 %copy-start.17 = (f32[2]{0:T(128)S(1)}, f32[2]{0:T(128)}, u32[]{:S(2)}) copy-start(f32[2]{0:T(128)} %param.33) | copy-start | bytes 28
  525.8 1.3 collective-permute-start
Sparse Core Ops, SparseCore 0:
  9.8 46.5 all-gather.9
  64.4 71.0 all-gather.7
  137.1 62.2 all-gather.5
  301.8 85.8 all-reduce.3
  423.4 43.9 reduce-scatter.3
  482.9 41.9 all-reduce.5
where the time goes:
time: 553 us; the launch traced here: 552 us
  waiting for transfers between devices  289 us (52%)
  matrix products  85.7 us (15%)
  blocking collectives  68.6 us (12%)
  other arithmetic  47.8 us (9%)
  local copies, waits for them, and re-layouts  45.9 us (8%)
  between operations  14.5 us (3%)
    psum x1, waiting for transfers between devices, per_device(): lax.psum(attn_part.astype(jnp.bfloat16), 'blk').astype(jnp.float32)  85.9 us
    all_gather x1, waiting for transfers between devices, per_device(): key_piece = lax.all_gather(keys_img, 'seq', axis=1, tiled=True)  59.2 us
    all_gather x1, waiting for transfers between devices, per_device(): lax.all_gather(img_hidden[0], 'blk', axis=2, tiled=True)  46.8 us
    unnamed x7, waiting for transfers between devices  44 us
    psum x1, waiting for transfers between devices, per_device(): lax.psum(velocity_part.astype(jnp.bfloat16), 'blk').astype(jnp.float32)  42.1 us
    dot_general x8, matrix products, project(): result = jnp.dot(flat_rows, weight, preferred_element_type=jnp.float32)  37 us
    dot_general x5, matrix products, attend_block(): jnp.einsum('pqhe,pkhe->phqk', query_heads, key_heads, preferred_element_t...  35.9 us
    reduce_sum x5, other arithmetic, attend_block(): denominator = denominator * factor + jnp.sum(weights, axis=-1)  30.6 us
  transfers between devices with their start and end apart: 7, of which 7 were waited for; matrix products, arithmetic and copies ran while one was open for 5% of the time, Pallas kernels for 0%

commit v1 on v0

--- a/solution.py
+++ b/solution.py
@@ -2,11 +2,16 @@
 import jax.numpy as jnp
 from jax import lax
 from jax.sharding import PartitionSpec as P
+from jax.lax import all_gather
 
 HEAD = 64
 STEPS = 28
 EPSILON = 1e-06
 BLOCK_ROWS = 512
+
+
+def resolve_set(u_in):
+    return all_gather(u_in, "blk").sum(axis=0)
 
 
 def from_partner(value, axis, bit):
@@ -136,7 +141,7 @@
     attended = (accumulated / denominator[..., None]).astype(jnp.bfloat16)
     attended = attended.transpose(0, 2, 1, 3).reshape(prompts, img_rows, head_width)
     attn_part = project(attended, w_out)
-    attn_sum = lax.psum(attn_part.astype(jnp.bfloat16), "blk").astype(jnp.float32)
+    attn_sum = resolve_set(attn_part.astype(jnp.bfloat16)).astype(jnp.float32)
     resid_full = (image_full.astype(jnp.float32) + image_mod[:, 2][:, None, :] * attn_sum).astype(
         jnp.bfloat16
     )

time: 553 us -> 598 us (1.081)
  waiting for transfers between devices: 289 us -> 324 us
  other arithmetic: 47.8 us -> 56.9 us
    all_gather x0 -> x1, waiting for transfers between devices: none -> 121 us  [resolve_set(): return all_gather(u_in, 'blk').sum(axis=0)]
    psum x1 -> x0, waiting for transfers between devices: 85.9 us -> none  [per_device(): lax.psum(attn_part.astype(jnp.bfloat16), 'blk').astype(jnp.float32)]
    reduce_sum x0 -> x1, other arithmetic: none -> 9.08 us  [resolve_set(): return all_gather(u_in, 'blk').sum(axis=0)]
  transfers between devices with their start and end apart: 7 -> 7, of which waited for: 7 -> 7; matrix products, arithmetic and copies ran while one was open for 5% -> 4% of each run, Pallas kernels for 0% -> 0%
where the time goes in v1:
time: 598 us; the launch traced here: 596 us
  waiting for transfers between devices  324 us (54%)
  matrix products  85.4 us (14%)
  blocking collectives  68.5 us (11%)
  other arithmetic  56.9 us (10%)
  local copies, waits for them, and re-layouts  45.9 us (8%)
  between operations  14.5 us (2%)
    all_gather x1, waiting for transfers between devices, resolve_set(): return all_gather(u_in, 'blk').sum(axis=0)  121 us
    all_gather x1, waiting for transfers between devices, per_device(): key_piece = lax.all_gather(keys_img, 'seq', axis=1, tiled=True)  59.2 us
    all_gather x1, waiting for transfers between devices, per_device(): lax.all_gather(img_hidden[0], 'blk', axis=2, tiled=True)  46.8 us
    unnamed x7, waiting for transfers between devices  43.8 us
    psum x1, waiting for transfers between devices, per_device(): lax.psum(velocity_part.astype(jnp.bfloat16), 'blk').astype(jnp.float32)  42.1 us
    dot_general x8, matrix products, project(): result = jnp.dot(flat_rows, weight, preferred_element_type=jnp.float32)  36.7 us
    dot_general x5, matrix products, attend_block(): jnp.einsum('pqhe,pkhe->phqk', query_heads, key_heads, preferred_element_t...  35.9 us
    reduce_sum x5, other arithmetic, attend_block(): denominator = denominator * factor + jnp.sum(weights, axis=-1)  30.6 us
  transfers between devices with their start and end apart: 7, of which 7 were waited for; matrix products, arithmetic and copies ran while one was open for 4% of the time, Pallas kernels for 0%

profile of v1, /device:TPU:0, one launch (start us, length us, event | category | flops | bytes accessed | tf_op | source)
XLA Modules:
  0.0 596.1 jit_solution(17292837516544759877)
XLA Ops:
  8.0 0.9 copy.69
  9.6 46.8 %all-gather.12.cloned.1.call-done = bf16[1,2,512,1536]{3,2,1,0:T(8,128)(2,1)} async-done(((bf16[1,2,512,384]{3,2,1,0:T(8,128)(2,1)}), bf16[1,2,512,1536]{3,2,1,0:T(8,128)(2,1)}) %all-gather.12.cloned.1.call-update) | async-done | bytes 3145744 | tf_op jit(solution)/shard_map/all_gather | solution.py:73
  56.4 2.5 convert_reduce_fusion
  59.2 1.0 fusion.18
  60.2 4.0 convolution_convert_fusion.1
  64.4 5.0 convolution_convert_fusion.3
  69.5 9.2 %all-gather.1 = bf16[1,2,40,1536]{3,2,1,0:T(8,128)(2,1)S(1)} all-gather(bf16[1,2,40,384]{3,2,1,0:T(8,128)(2,1)S(1)} %copy-done.12), channel_id=3, replica_groups=mesh['cfg'=2,'seq'=4,'blk'=4] {'blk'}, dimensions={3}, use_global_device_ids=true | all-gather | bytes 307200 | tf_op jit(solution)/shard_map/all_gather | solution.py:74
  79.1 1.7 fusion.79
  80.8 16.4 %all_gather.28 = bf16[2,160,384]{2,1,0:T(8,128)(2,1)} all-gather(bf16[2,40,384]{2,1,0:T(8,128)(2,1)S(1)} %fusion.79), channel_id=1, replica_groups=mesh['cfg'=2,'seq'=4,'blk'=4] {'seq'}, dimensions={1}, use_global_device_ids=true | all-gather | bytes 307200 | tf_op jit(solution)/shard_map/all_gather | solution.py:133
  97.2 1.1 copy.39
  98.3 1.7 fusion.82
  100.0 16.6 %all_gather.29 = bf16[2,160,384]{2,1,0:T(8,128)(2,1)S(1)} all-gather(bf16[2,40,384]{2,1,0:T(8,128)(2,1)S(1)} %fusion.82), channel_id=1, replica_groups=mesh['cfg'=2,'seq'=4,'blk'=4] {'seq'}, dimensions={1}, use_global_device_ids=true | all-gather | bytes 307200 | tf_op jit(solution)/shard_map/all_gather | solution.py:134
  116.6 0.9 copy.40
  117.6 4.0 convolution_convert_fusion.2
  121.6 0.9 copy-done.2
  122.5 3.4 fusion.41
  125.9 9.6 %all-gather.10.cloned.1.call-done = bf16[2,2048,384]{2,1,0:T(8,128)(2,1)} async-done(((bf16[2,512,384]{2,1,0:T(8,128)(2,1)}), bf16[2,2048,384]{2,1,0:T(8,128)(2,1)}) %all-gather.10.cloned.1.call-update) | async-done | bytes 3145744 | tf_op jit(solution)/shard_map/all_gather | solution.py:121
  135.5 4.7 copy.38
  140.2 59.2 %all-gather.8.cloned.1.call-done = bf16[2,2048,384]{2,1,0:T(8,128)(2,1)} async-done(((bf16[2,512,384]{2,1,0:T(8,128)(2,1)}), bf16[2,2048,384]{2,1,0:T(8,128)(2,1)}) %all-gather.8.cloned.1.call-update) | async-done | bytes 3145744 | tf_op jit(solution)/shard_map/all_gather | solution.py:120
  199.4 4.7 copy.36
  204.1 87.5 %while.15 = (s32[]{:T(128)}, f32[2,6,512,64]{2,3,1,0:T(8,128)S(1)}, f32[2,6,512]{2,1,0:T(8,128)}, f32[2,6,512]{2,1,0:T(8,128)}, bf16[4,2,512,384]{2,3,1,0:T(8,12...) while((s32[]{:T(128)}, f32[2,6,512,64]{2,3,1,0:T(8,128)S(1)}, ...), condition=%wide.region_5.0_spmd.clone, body=%wide.region_2.5_spmd.clone.sunk | while | flops 831682560 | bytes 97419496 | solution.py:131
  204.1 1.5 constant_dynamic-slice_fusion.5
  205.5 8.1 %bitcast_reduce_fusion.2 = (f32[2,6,512]{2,1,0:T(8,128)}, f32[2,6,512,512]{3,2,1,0:T(8,128)}) fusion(bf16[2,512,6,64]{1,3,2,0:T(8,128)(2,1)S(1)} %bitcast.166, bf16[2,512,6,64]{1,3,2,0:T(8,128)(2,1)} %get-tuple-element.199), kind=kOutput, calls=%fused_computation.1.clone.1 | convolution fusion | flops 408938496 | bytes 14180352 | tf_op jit(solution)/shard_map/while/body/eval_jaxpr/pqhe,pkhe->phqk/dot_general | solution.py:96
  214.4 6.8 %fusion.134 = f32[2,6,512]{2,1,0:T(8,128)S(1)} fusion(f32[2,6,512,512]{3,2,1,0:T(8,128)} %get-tuple-element.172, f32[2,6,512]{2,1,0:T(8,128)S(1)} %select_maximum_fusion.2), kind=kLoop, calls=%fused_computation.3.clone.1 | loop fusion | flops 9431040 | bytes 12632064 | tf_op jit(solution)/shard_map/while/body/eval_jaxpr/reduce_sum | solution.py:104
  221.3 1.3 copy-done.1
  222.6 2.7 fusion.136
  225.9 1.5 constant_dynamic-slice_fusion.5
  227.4 8.1 %bitcast_reduce_fusion.2 = (f32[2,6,512]{2,1,0:T(8,128)}, f32[2,6,512,512]{3,2,1,0:T(8,128)}) fusion(bf16[2,512,6,64]{1,3,2,0:T(8,128)(2,1)S(1)} %bitcast.166, bf16[2,512,6,64]{1,3,2,0:T(8,128)(2,1)} %get-tuple-element.199), kind=kOutput, calls=%fused_computation.1.clone.1 | convolution fusion | flops 408938496 | bytes 14180352 | tf_op jit(solution)/shard_map/while/body/eval_jaxpr/pqhe,pkhe->phqk/dot_general | solution.py:96
  236.3 6.8 %fusion.134 = f32[2,6,512]{2,1,0:T(8,128)S(1)} fusion(f32[2,6,512,512]{3,2,1,0:T(8,128)} %get-tuple-element.172, f32[2,6,512]{2,1,0:T(8,128)S(1)} %select_maximum_fusion.2), kind=kLoop, calls=%fused_computation.3.clone.1 | loop fusion | flops 9431040 | bytes 12632064 | tf_op jit(solution)/shard_map/while/body/eval_jaxpr/reduce_sum | solution.py:104
  243.2 1.3 copy-done.1
  244.5 2.7 fusion.136
  247.8 1.5 constant_dynamic-slice_fusion.5
  249.3 8.1 %bitcast_reduce_fusion.2 = (f32[2,6,512]{2,1,0:T(8,128)}, f32[2,6,512,512]{3,2,1,0:T(8,128)}) fusion(bf16[2,512,6,64]{1,3,2,0:T(8,128)(2,1)S(1)} %bitcast.166, bf16[2,512,6,64]{1,3,2,0:T(8,128)(2,1)} %get-tuple-element.199), kind=kOutput, calls=%fused_computation.1.clone.1 | convolution fusion | flops 408938496 | bytes 14180352 | tf_op jit(solution)/shard_map/while/body/eval_jaxpr/pqhe,pkhe->phqk/dot_general | solution.py:96
  257.4 0.8 select_maximum_fusion.2
  258.2 6.8 %fusion.134 = f32[2,6,512]{2,1,0:T(8,128)S(1)} fusion(f32[2,6,512,512]{3,2,1,0:T(8,128)} %get-tuple-element.172, f32[2,6,512]{2,1,0:T(8,128)S(1)} %select_maximum_fusion.2), kind=kLoop, calls=%fused_computation.3.clone.1 | loop fusion | flops 9431040 | bytes 12632064 | tf_op jit(solution)/shard_map/while/body/eval_jaxpr/reduce_sum | solution.py:104
  265.1 1.3 copy-done.1
  266.4 2.7 fusion.136
  269.7 1.5 constant_dynamic-slice_fusion.5
  271.2 8.1 %bitcast_reduce_fusion.2 = (f32[2,6,512]{2,1,0:T(8,128)}, f32[2,6,512,512]{3,2,1,0:T(8,128)}) fusion(bf16[2,512,6,64]{1,3,2,0:T(8,128)(2,1)S(1)} %bitcast.166, bf16[2,512,6,64]{1,3,2,0:T(8,128)(2,1)} %get-tuple-element.199), kind=kOutput, calls=%fused_computation.1.clone.1 | convolution fusion | flops 408938496 | bytes 14180352 | tf_op jit(solution)/shard_map/while/body/eval_jaxpr/pqhe,pkhe->phqk/dot_general | solution.py:96
  279.3 0.8 select_maximum_fusion.2
  280.1 6.8 %fusion.134 = f32[2,6,512]{2,1,0:T(8,128)S(1)} fusion(f32[2,6,512,512]{3,2,1,0:T(8,128)} %get-tuple-element.172, f32[2,6,512]{2,1,0:T(8,128)S(1)} %select_maximum_fusion.2), kind=kLoop, calls=%fused_computation.3.clone.1 | loop fusion | flops 9431040 | bytes 12632064 | tf_op jit(solution)/shard_map/while/body/eval_jaxpr/reduce_sum | solution.py:104
  287.0 1.3 copy-done.1
  288.3 2.7 fusion.136
  291.6 0.9 max.8
  292.5 3.4 fusion.47
  295.9 2.2 divide_convert_fusion
  298.1 3.5 convolution_convert_fusion
  302.0 121.0 %all-gather.14.cloned.1.call-done = bf16[8,512,1536]{2,1,0:T(8,128)(2,1)} async-done(((bf16[2,512,1536]{2,1,0:T(8,128)(2,1)}), bf16[8,512,1536]{2,1,0:T(8,128)(2,1)}) %all-gather.14.cloned.1.call-update) | async-done | bytes 12582928 | tf_op jit(solution)/shard_map/all_gather | solution.py:14
  423.0 9.1 %reduce_sum.107 = bf16[2,512,1536]{2,1,0:T(8,128)(2,1)} reduce(bf16[4,2,512,1536]{3,2,1,0:T(8,128)(2,1)} %bitcast.171, bf16[]{:T(256)} %constant.75.clone.1), dimensions={0}, to_apply=%region_10.11 | reduce | flops 4718592 | bytes 15728642 | tf_op jit(solution)/shard_map/reduce_sum | solution.py:14
  432.1 4.0 convert_reduce_fusion.1
  436.1 1.6 copy-done.4
  437.8 1.0 fusion.22
  438.7 15.6 %fusion.38 = bf16[2,512,1536]{2,1,0:T(8,128)(2,1)} fusion(bf16[1536,1536]{1,0:T(8,128)(2,1)} %param.27, bf16[1536,1536]{1,0:T(8,128)(2,1)} %param.26, bf16[2,512,1536]{2,1,0:T(8,128)(2,1)} %copy-done.4, f32[2,1536]{1,0:T(2,128)S(1)} %get-tuple-element.113, f32[2,1536]{1,0:T(2,128)S(1)} %get-tuple-element.114, f32[2,512]{1,0:T(2,128)S(1)} %add_rsqrt_fusion.1, ...), kind=kOutput, calls=%fused_computation.50 | convolution fusion | flops 9688842240 | bytes 15761408 | tf_op jit(solution)/shard_map/dot_general | solution.py:36
  454.4 8.7 %copy.44 = bf16[2,512,1536]{1,0,2:T(2,128)(2,1)} copy(bf16[2,512,1536]{2,1,0:T(8,128)(2,1)} %fusion.38) | data formatting | bytes 6291456
  463.0 4.4 copy.57
  468.6 43.0 %reduce-scatter.4.cloned.1.call-done = bf16[384,1024]{1,0:T(8,128)(2,1)} async-done(((bf16[1536,1024]{1,0:T(8,128)(2,1)}), bf16[384,1024]{1,0:T(8,128)(2,1)}) %reduce-scatter.4.cloned.1.call-update) | async-done | bytes 786448
  511.6 2.6 reshape.159
  514.9 1.7 convert_reduce_fusion.2
  516.5 9.1 %all-reduce = (f32[2,512]{1,0:T(2,128)S(1)}, f32[2,512]{1,0:T(2,128)S(1)}) all-reduce(f32[2,512]{1,0:T(2,128)S(1)} %get-tuple-element.69, f32[2,512]{1,0:T(2,128)S(1)} %get-tuple-element.68), channel_id=1, replica_groups=mesh['cfg'=2,'seq'=4,'blk'=4] {'blk'}, use_global_device_ids=true, to_apply=%region_17.18 | all-reduce | flops 2048 | bytes 16384 | tf_op jit(solution)/shard_map/psum | solution.py:159
  525.7 1.2 convolution_convert_fusion.4
  526.9 42.1 %all-reduce.3.cloned.1.call-done = bf16[2,512,64]{1,2,0:T(8,128)(2,1)} async-done(((bf16[2,512,64]{1,2,0:T(8,128)(2,1)}), bf16[2,512,64]{1,2,0:T(8,128)(2,1)}) %all-reduce.3.cloned.1.call-update) | async-done | bytes 131088 | tf_op jit(solution)/shard_map/psum | solution.py:177
  569.0 0.9 convert_element_type.119
  570.1 1.2 collective-permute-done
  572.0 17.2 %pmax.7 = f32[2]{0:T(128)} all-reduce(f32[2]{0:T(128)S(1)} %get-tuple-element.97), channel_id=1, replica_groups=mesh['cfg'=2,'seq'=4,'blk'=4] {'cfg','seq'}, use_global_device_ids=true, to_apply=%region_20.21 | all-reduce | flops 2 | bytes 16 | tf_op jit(solution)/shard_map/pmax | solution.py:188
  (115 shorter events, 9.6 us)
Async XLA Ops:
  7.2 291.0 %copy-start = (bf16[384,1536]{1,0:T(8,128)(2,1)S(1)}, bf16[384,1536]{1,0:T(8,128)(2,1)}, u32[]{:S(2)}) copy-start(bf16[384,1536]{1,0:T(8,128)(2,1)} %param.25) | copy-start | bytes 3538948
  7.2 49.2 %all-gather.12.cloned.1.call-start = ((), (), s32[]{:S(2)}) async-start(), calls=%async_computation.4 | async-start | bytes 3932160 | tf_op jit(solution)/shard_map/all_gather | solution.py:73
  7.9 127.6 %all-gather.10.cloned.1.call-start = ((), (), s32[]{:S(2)}) async-start(), calls=%async_computation.2 | async-start | bytes 3932160 | tf_op jit(solution)/shard_map/all_gather | solution.py:121
  56.4 2.8 copy-start.3
  64.3 5.2 copy-start.12
  64.3 14.7 %copy-start.15 = (f32[1,2,2,1536]{3,2,1,0:T(2,128)S(1)}, f32[1,2,2,1536]{3,2,1,0:T(2,128)}, u32[]{:S(2)}) copy-start(f32[1,2,2,1536]{3,2,1,0:T(2,128)} %param.21) | copy-start | bytes 73732
  64.3 135.0 %all-gather.8.cloned.1.call-start = ((), (), s32[]{:S(2)}) async-start(), calls=%async_computation.1 | async-start | bytes 3932160 | tf_op jit(solution)/shard_map/all_gather | solution.py:120
  69.3 48.2 %copy-start.19 = (s32[1,2]{1,0:T(1,128)S(1)}, s32[1,2]{1,0:T(1,128)}, u32[]{:S(2)}) copy-start(s32[1,2]{1,0:T(1,128)} %param.30) | copy-start | bytes 28
  69.4 353.6 %all-gather.14.cloned.1.call-start = ((), (), s32[]{:S(2)}) async-start(), calls=%async_computation.5 | async-start | bytes 15728640 | tf_op jit(solution)/shard_map/all_gather | solution.py:14
  121.6 0.9 copy-start.2
  214.4 6.9 %copy-start.6 = (f32[2,6,512]{2,1,0:T(8,128)S(1)}, f32[2,6,512]{2,1,0:T(8,128)}, u32[]{:S(2)}) copy-start(f32[2,6,512]{2,1,0:T(8,128)} %get-tuple-element.187) | copy-start | bytes 73732 | tf_op jit(solution)/shard_map/while
  214.4 6.9 %copy-start.8 = (f32[2,6,512]{2,1,0:T(8,128)S(1)}, f32[2,6,512]{2,1,0:T(8,128)}, u32[]{:S(2)}) copy-start(f32[2,6,512]{2,1,0:T(8,128)} %get-tuple-element.188) | copy-start | bytes 73732 | tf_op jit(solution)/shard_map/while
  214.4 8.2 %copy-start.1 = (f32[2,6,512,512]{3,2,1,0:T(8,128)S(1)}, f32[2,6,512,512]{3,2,1,0:T(8,128)}, u32[]{:S(2)}) copy-start(f32[2,6,512,512]{3,2,1,0:T(8,128)} %get-tuple-element.172) | copy-start | bytes 37748740 | tf_op jit(solution)/shard_map/while
  221.3 4.0 copy-start.9
  236.3 6.8 %copy-start.6 = (f32[2,6,512]{2,1,0:T(8,128)S(1)}, f32[2,6,512]{2,1,0:T(8,128)}, u32[]{:S(2)}) copy-start(f32[2,6,512]{2,1,0:T(8,128)} %get-tuple-element.187) | copy-start | bytes 73732 | tf_op jit(solution)/shard_map/while
  236.3 6.9 %copy-start.8 = (f32[2,6,512]{2,1,0:T(8,128)S(1)}, f32[2,6,512]{2,1,0:T(8,128)}, u32[]{:S(2)}) copy-start(f32[2,6,512]{2,1,0:T(8,128)} %get-tuple-element.188) | copy-start | bytes 73732 | tf_op jit(solution)/shard_map/while
  236.3 8.2 %copy-start.1 = (f32[2,6,512,512]{3,2,1,0:T(8,128)S(1)}, f32[2,6,512,512]{3,2,1,0:T(8,128)}, u32[]{:S(2)}) copy-start(f32[2,6,512,512]{3,2,1,0:T(8,128)} %get-tuple-element.172) | copy-start | bytes 37748740 | tf_op jit(solution)/shard_map/while
  243.2 4.0 copy-start.9
  258.2 6.8 %copy-start.6 = (f32[2,6,512]{2,1,0:T(8,128)S(1)}, f32[2,6,512]{2,1,0:T(8,128)}, u32[]{:S(2)}) copy-start(f32[2,6,512]{2,1,0:T(8,128)} %get-tuple-element.187) | copy-start | bytes 73732 | tf_op jit(solution)/shard_map/while
  258.2 6.9 %copy-start.8 = (f32[2,6,512]{2,1,0:T(8,128)S(1)}, f32[2,6,512]{2,1,0:T(8,128)}, u32[]{:S(2)}) copy-start(f32[2,6,512]{2,1,0:T(8,128)} %get-tuple-element.188) | copy-start | bytes 73732 | tf_op jit(solution)/shard_map/while
  258.2 8.2 %copy-start.1 = (f32[2,6,512,512]{3,2,1,0:T(8,128)S(1)}, f32[2,6,512,512]{3,2,1,0:T(8,128)}, u32[]{:S(2)}) copy-start(f32[2,6,512,512]{3,2,1,0:T(8,128)} %get-tuple-element.172) | copy-start | bytes 37748740 | tf_op jit(solution)/shard_map/while
  265.1 4.0 copy-start.9
  280.1 6.8 %copy-start.6 = (f32[2,6,512]{2,1,0:T(8,128)S(1)}, f32[2,6,512]{2,1,0:T(8,128)}, u32[]{:S(2)}) copy-start(f32[2,6,512]{2,1,0:T(8,128)} %get-tuple-element.187) | copy-start | bytes 73732 | tf_op jit(solution)/shard_map/while
  280.1 6.9 %copy-start.8 = (f32[2,6,512]{2,1,0:T(8,128)S(1)}, f32[2,6,512]{2,1,0:T(8,128)}, u32[]{:S(2)}) copy-start(f32[2,6,512]{2,1,0:T(8,128)} %get-tuple-element.188) | copy-start | bytes 73732 | tf_op jit(solution)/shard_map/while
  280.1 8.2 %copy-start.1 = (f32[2,6,512,512]{3,2,1,0:T(8,128)S(1)}, f32[2,6,512,512]{3,2,1,0:T(8,128)}, u32[]{:S(2)}) copy-start(f32[2,6,512,512]{3,2,1,0:T(8,128)} %get-tuple-element.172) | copy-start | bytes 37748740 | tf_op jit(solution)/shard_map/while
  287.0 4.0 copy-start.9
  291.6 4.3 copy-start.7
  291.6 4.3 copy-start.10
  291.6 4.3 copy-start.5
  298.1 3.8 copy-start.13
  298.1 3.8 copy-start.14
  301.6 210.0 %reduce-scatter.4.cloned.1.call-start = ((), (), s32[]{:S(2)}) async-start(), calls=%async_computation.6 | async-start | bytes 3932160
  436.1 1.7 copy-start.4
  463.0 5.5 copy-start.16
  467.4 58.2 %copy-start.18 = (bf16[384,64]{0,1:T(8,128)(2,1)S(1)}, bf16[384,64]{0,1:T(8,128)(2,1)}, u32[]{:S(2)}) copy-start(bf16[384,64]{0,1:T(8,128)(2,1)} %param.28) | copy-start | bytes 147460
  467.5 101.5 %all-reduce.3.cloned.1.call-start = ((), (), s32[]{:S(2)}) async-start(), calls=%async_computation.3 | async-start | bytes 262144 | tf_op jit(solution)/shard_map/psum | solution.py:177
  468.6 101.5 %copy-start.20 = (s32[2]{0:T(128)S(1)}, s32[2]{0:T(128)}, u32[]{:S(2)}) copy-start(s32[2]{0:T(128)} %param.31) | copy-start | bytes 28
  468.6 101.5 %copy-start.21 = (s32[2]{0:T(128)S(1)}, s32[2]{0:T(128)}, u32[]{:S(2)}) copy-start(s32[2]{0:T(128)} %param.32) | copy-start | bytes 28
  468.6 102.7 %copy-start.11 = (f32[2,512,32]{1,2,0:T(8,128)S(1)}, f32[2,512,32]{1,2,0:T(8,128)}, u32[]{:S(2)}) copy-start(f32[2,512,32]{1,2,0:T(8,128)} %param.29) | copy-start | bytes 393220
  468.6 102.7 %copy-start.17 = (f32[2]{0:T(128)S(1)}, f32[2]{0:T(128)}, u32[]{:S(2)}) copy-start(f32[2]{0:T(128)} %param.33) | copy-start | bytes 28
  569.9 1.3 collective-permute-start
Sparse Core Ops, SparseCore 0:
  9.8 46.5 all-gather.11
  64.4 71.0 all-gather.9
  137.1 62.2 all-gather.7
  301.8 121.1 all-gather.13
  467.6 43.9 reduce-scatter.3
  527.0 41.9 all-reduce.2
